TPU v7x, 256 devices: a whole 4x4x8 slice. The times are simulated.
256 devices in a mesh: pool: 32 (over y, x, z_hi), tp: 8 (over z_lo, core).
Axes of the slice: x: 4, y: 4, z: 8 (z_hi: 2, z_lo: 4; z = z_hi * 4 + z_lo), core: 2. Of those that a mesh axis runs over, the one named last changes fastest.
Arguments:
- queries: bfloat16 [2, 4096, 8192], P(None, 'pool', 'tp'), may hold values from -24 to 24
- new_kv: bfloat16 [2, 8, 2, 4096, 128], P(None, 'tp', None, 'pool'), may hold values from -6 to 6
- kv_pool: bfloat16 [96, 8, 2, 128, 128], P('pool', 'tp'), may hold values from -6 to 6
- block_owner: int32 [2, 48], replicated, may hold values from 0 to 31, as said below
- block_slot: int32 [2, 48], replicated, may hold values from 0 to 2
- prefix_len: int32 [2], replicated, may hold values from 1921 to 6144, as said below
- decode_page: int32 [2, 32], replicated, may hold values from 0 to 63, as said below
- out_weight: bfloat16 [8192, 4096], P('tp'), may hold values from -1 to 1
Outputs:
- attn_out: bfloat16 [2, 4096, 4096], P(None, 'pool', 'tp')
- decode_cache: bfloat16 [64, 8, 2, 128, 128], P('pool', 'tp')
Inputs may be any that keep to these rules, and one draw needn't show every extreme that they name: block_owner[r, j] and block_slot[r, j] together name row block_owner[r, j] * 3 + block_slot[r, j] of kv_pool, and every row of kv_pool is named exactly once. Of the rows named by entries j with j * 128 < prefix_len[r], every pool device holds exactly 2. `prefix_len`: one request's prefix is 6144 tokens long. `decode_page`: each of the 64 decode pages is named exactly once.
All inputs are finite; a program needn't handle non-finite values.
Results may differ from a plain program's by a relative error of at most 0.02.
Values may be sent and summed in bfloat16 or wider, within the bound.
A program may use at most 64 MiB of HBM per device.

v0:
```python
import math

import jax
import jax.numpy as jnp
from jax import lax
from jax.sharding import PartitionSpec as P


def absorb(carry_state, query_rows, key_rows, value_rows, visible, score_scale):
    row_max, row_total, weighted = carry_state
    scores = (
        jnp.einsum("grd,gkd->grk", query_rows, key_rows, preferred_element_type=jnp.float32)
        * score_scale
    )
    scores = jnp.where(visible[None], scores, -jnp.inf)
    new_max = jnp.maximum(row_max, jnp.max(scores, axis=2))
    factor = jnp.exp(row_max - new_max)
    weights = jnp.exp(scores - new_max[:, :, None])
    row_total = row_total * factor + jnp.sum(weights, axis=2)
    weighted = weighted * factor[:, :, None] + jnp.einsum(
        "grk,gkd->grd", weights.astype(jnp.bfloat16), value_rows, preferred_element_type=jnp.float32
    )
    return (new_max, row_total, weighted)


def shards(queries, new_kv, kv_pool, block_owner, block_slot, prefix_len, decode_page, out_weight):
    pool_count = lax.axis_size("pool")
    me_index = lax.axis_index("pool")
    requests, tok_local, query_width = queries.shape
    kv_local = new_kv.shape[1]
    head_dim = new_kv.shape[4]
    page_len = kv_pool.shape[3]
    pool_local = kv_pool.shape[0]
    block_total = block_owner.shape[1]
    group_size = query_width // (kv_local * head_dim)
    row_count = tok_local * group_size
    new_total = tok_local * pool_count
    score_scale = 1.0 / math.sqrt(head_dim)
    gathered_new = lax.all_gather(new_kv, "pool", axis=3, tiled=True)
    pool_pages = lax.all_gather(kv_pool, "pool", axis=0, tiled=True)
    page_index = block_owner * pool_local + block_slot
    query_all = queries.reshape(requests, tok_local, kv_local, group_size, head_dim)
    row_pos = me_index * tok_local + jnp.arange(row_count, dtype=jnp.int32) // group_size
    pages_per_block = math.gcd(block_total, max(1, 1024 // page_len))
    prefix_blocks = block_total // pages_per_block
    prefix_keys = pages_per_block * page_len
    new_block = math.gcd(new_total, 1024)
    new_blocks = new_total // new_block
    outputs = []
    for request in range(requests):
        query_rows = jnp.transpose(query_all[request], (1, 0, 2, 3)).reshape(
            kv_local, row_count, head_dim
        )
        length = prefix_len[request]
        page_list = page_index[request]
        own_new = gathered_new[request]
        start_state = (
            jnp.full((kv_local, row_count), -1e30, jnp.float32),
            jnp.zeros((kv_local, row_count), jnp.float32),
            jnp.zeros((kv_local, row_count, head_dim), jnp.float32),
        )

        def prefix_step(carry_state, block_id):
            picked = lax.dynamic_slice_in_dim(
                page_list, block_id * pages_per_block, pages_per_block
            )
            page_block = jnp.take(pool_pages, picked, axis=0)
            key_rows = jnp.moveaxis(page_block[:, :, 0], 1, 0).reshape(
                kv_local, prefix_keys, head_dim
            )
            value_rows = jnp.moveaxis(page_block[:, :, 1], 1, 0).reshape(
                kv_local, prefix_keys, head_dim
            )
            positions = block_id * prefix_keys + jnp.arange(prefix_keys, dtype=jnp.int32)
            visible = jnp.broadcast_to((positions < length)[None, :], (row_count, prefix_keys))
            carry_state = absorb(
                carry_state, query_rows, key_rows, value_rows, visible, score_scale
            )
            return (carry_state, None)

        def new_step(carry_state, block_id):
            new_slice = lax.dynamic_slice_in_dim(own_new, block_id * new_block, new_block, axis=2)
            positions = block_id * new_block + jnp.arange(new_block, dtype=jnp.int32)
            visible = positions[None, :] <= row_pos[:, None]
            carry_state = absorb(
                carry_state, query_rows, new_slice[:, 0], new_slice[:, 1], visible, score_scale
            )
            return (carry_state, None)

        carry_state, unused = lax.scan(
            prefix_step, start_state, jnp.arange(prefix_blocks, dtype=jnp.int32)
        )
        carry_state, unused = lax.scan(
            new_step, carry_state, jnp.arange(new_blocks, dtype=jnp.int32)
        )
        row_max, row_total, weighted = carry_state
        mixed_rows = (weighted / row_total[:, :, None]).astype(jnp.bfloat16)
        mixed_rows = jnp.transpose(
            mixed_rows.reshape(kv_local, tok_local, group_size, head_dim), (1, 0, 2, 3)
        )
        outputs.append(mixed_rows.reshape(tok_local, query_width))
    attention = jnp.stack(outputs).reshape(requests * tok_local, query_width)
    partial_sums = jnp.dot(attention, out_weight, preferred_element_type=jnp.float32)
    summed = lax.psum_scatter(
        partial_sums.astype(jnp.bfloat16), "tp", scatter_dimension=1, tiled=True
    )
    attn_out = summed.reshape(requests, tok_local, -1)
    pages_here = requests * tok_local // page_len
    page_count = new_total // page_len
    slot_global = me_index * pages_here + jnp.arange(pages_here, dtype=jnp.int32)
    flat_page = decode_page.reshape(-1)
    matches = flat_page[None, :] == slot_global[:, None]
    source = jnp.sum(
        jnp.where(matches, jnp.arange(flat_page.shape[0], dtype=jnp.int32)[None, :], 0), axis=1
    )
    paged = gathered_new.reshape(requests, kv_local, 2, page_count, page_len, head_dim)
    decode_cache = paged[source // page_count, :, :, source % page_count]
    return (attn_out, decode_cache)


def solution(mesh):
    return jax.shard_map(
        shards,
        mesh=mesh,
        in_specs=(
            P(None, "pool", "tp"),
            P(None, "tp", None, "pool", None),
            P("pool", "tp", None, None, None),
            P(),
            P(),
            P(),
            P(),
            P("tp", None),
        ),
        out_specs=(P(None, "pool", "tp"), P("pool", "tp", None, None, None)),
        check_vma=False,
    )
```

profile of v0, /device:TPU:24, one launch (start us, length us, event | category | flops | bytes accessed | tf_op | source)
XLA Modules:
  0.0 481.7 jit_solution(15204114758598374586)
XLA Ops:
  8.8 1.1 fusion.95
  10.1 1.3 fusion.96
  12.1 112.6 %all-gather.5.cloned.1.call-done = bf16[2,1,2,4096,128]{4,3,2,1,0:T(8,128)(2,1)} async-done(((bf16[2,1,2,128,128]{4,3,2,1,0:T(8,128)(2,1)}), bf16[2,1,2,4096,128]{4,3,2,1,0:T(8,128)(2,1)}) %all-gather.5.cloned.1.call-update) | async-done | bytes 4194320 | tf_op jit(solution)/shard_map/all_gather | solution.py:39
  124.7 3.8 slice_bitcast_fusion.1
  128.5 127.2 %all-gather.3.cloned.1.call-done = bf16[96,1,2,128,128]{4,3,2,1,0:T(8,128)(2,1)} async-done(((bf16[3,1,2,128,128]{4,3,2,1,0:T(8,128)(2,1)}), bf16[96,1,2,128,128]{4,3,2,1,0:T(8,128)(2,1)}) %all-gather.3.cloned.1.call-update) | async-done | bytes 6291472 | tf_op jit(solution)/shard_map/all_gather | solution.py:40
  255.8 63.8 %while.62 = (s32[]{:T(128)}, f32[1,1024]{1,0:T(1,128)S(1)}, f32[1,1024]{1,0:T(1,128)S(1)}, f32[1,1024,128]{2,1,0:T(8,128)}, s32[6]{0:T(128)S(1)}, /*index=5*/s32...) while((s32[]{:T(128)}, f32[1,1024]{1,0:T(1,128)S(1)}, ...), condition=%wide.region_3.5_spmd.clone, body=%wide.region_0.4_spmd.clone.sunk | while | flops 549068864 | bytes 21832116 | solution.py:90
  258.6 3.4 gather_fusion
  264.2 1.4 fusion.149
  269.3 3.4 gather_fusion
  274.8 1.4 fusion.149
  279.9 3.4 gather_fusion
  285.5 1.4 fusion.149
  290.5 3.4 gather_fusion
  294.1 1.0 fusion.145
  296.1 1.4 fusion.149
  301.2 3.4 gather_fusion
  306.7 1.4 fusion.149
  311.8 3.4 gather_fusion
  317.4 1.4 fusion.149
  319.6 63.2 %while.63 = (s32[]{:T(128)}, f32[1,1024]{1,0:T(1,128)S(1)}, f32[1,1024]{1,0:T(1,128)S(1)}, f32[1,1024,128]{2,1,0:T(8,128)}, s32[6]{0:T(128)S(1)}, /*index=5*/s32...) while((s32[]{:T(128)}, f32[1,1024]{1,0:T(1,128)S(1)}, ...), condition=%wide.region_11.13_spmd.clone, body=%wide.region_8.12_spmd.clone.sunk | while | flops 549068864 | bytes 21832116 | solution.py:90
  322.3 3.4 gather_fusion.1
  325.9 1.0 fusion.154
  327.9 1.4 fusion.158
  332.9 3.4 gather_fusion.1
  336.5 1.0 fusion.154
  338.4 1.4 fusion.158
  343.4 3.4 gather_fusion.1
  347.0 1.0 fusion.154
  349.0 1.4 fusion.158
  353.9 3.4 gather_fusion.1
  357.5 1.0 fusion.154
  359.5 1.4 fusion.158
  364.4 3.4 gather_fusion.1
  368.0 1.0 fusion.154
  370.0 1.4 fusion.158
  375.0 3.4 gather_fusion.1
  378.6 1.0 fusion.154
  380.5 1.4 fusion.158
  382.8 29.4 %while.60 = (s32[]{:T(128)}, f32[1,1024]{1,0:T(1,128)S(1)}, f32[1,1024]{1,0:T(1,128)S(1)}, f32[1,1024,128]{2,1,0:T(8,128)}, s32[4]{0:T(128)S(1)}, /*index=5*/bf1...) while((s32[]{:T(128)}, f32[1,1024]{1,0:T(1,128)S(1)}, ...), condition=%wide.region_7.9_spmd.clone, body=%wide.region_4.8_spmd.clone.sunk | while | flops 551825408 | bytes 18710808 | solution.py:93
  384.0 1.7 fusion.133
  385.8 1.0 fusion.134
  386.9 2.4 fusion.135
  391.4 1.7 fusion.133
  393.2 1.0 fusion.134
  394.2 2.4 fusion.135
  398.8 1.7 fusion.133
  400.5 1.0 fusion.134
  401.6 2.4 fusion.135
  406.1 1.7 fusion.133
  407.9 1.0 fusion.134
  409.0 2.4 fusion.135
  412.2 1.2 divide_convert_fusion.1
  413.6 18.0 %while.61 = (s32[]{:T(128)}, f32[1,1024]{1,0:T(1,128)S(1)}, f32[1,1024]{1,0:T(1,128)S(1)}, f32[1,1024,128]{2,1,0:T(8,128)S(1)}, s32[4]{0:T(128)S(1)}, /*index=5*...) while((s32[]{:T(128)}, f32[1,1024]{1,0:T(1,128)S(1)}, ...), condition=%wide.region_15.17_spmd.clone, body=%wide.region_12.16_spmd.clone.sunk | while | flops 551825408 | bytes 14516447 | solution.py:93
  415.8 1.0 fusion.139
  416.9 1.4 fusion.140
  420.3 1.0 fusion.139
  421.4 1.3 fusion.140
  424.8 1.0 fusion.139
  425.8 1.3 fusion.140
  429.2 1.0 fusion.139
  430.3 1.3 fusion.140
  432.1 7.1 %convolution_convert_fusion = bf16[256,4096]{1,0:T(8,128)(2,1)} fusion(bf16[256,1024]{1,0:T(8,128)(2,1)S(1)} %bitcast.268, bf16[1024,4096]{1,0:T(8,128)(2,1)} %param.25), kind=kOutput, calls=%fused_computation.111 | convolution fusion | flops 2148532224 | bytes 11010048 | tf_op jit(solution)/shard_map/dot_general | solution.py:103
  439.5 3.4 gather_fusion.2
  442.9 32.3 %reduce-scatter.2.cloned.1.call-done = bf16[256,512]{1,0:T(8,128)(2,1)} async-done(((bf16[256,4096]{1,0:T(8,128)(2,1)}), bf16[256,512]{1,0:T(8,128)(2,1)}) %reduce-scatter.2.cloned.1.call-update) | async-done | bytes 262160 | tf_op jit(solution)/shard_map/reduce_scatter | solution.py:104
  (265 shorter events, 58.7 us)
Async XLA Ops:
  7.2 117.5 %all-gather.5.cloned.1.call-start = ((), (), s32[]{:S(2)}) async-start(), calls=%async_computation.2 | async-start | bytes 4325376 | tf_op jit(solution)/shard_map/all_gather | solution.py:39
  7.9 247.9 %all-gather.3.cloned.1.call-start = ((), (), s32[]{:S(2)}) async-start(), calls=%async_computation.1 | async-start | bytes 6488064 | tf_op jit(solution)/shard_map/all_gather | solution.py:40
  8.6 466.5 %reduce-scatter.2.cloned.1.call-start = ((), (), s32[]{:S(2)}) async-start(), calls=%async_computation.3 | async-start | bytes 2359296 | tf_op jit(solution)/shard_map/reduce_scatter | solution.py:104
  262.2 2.0 copy-start.3
  265.6 0.8 copy-start.4
  272.9 2.0 copy-start.3
  276.2 0.8 copy-start.4
  283.5 2.0 copy-start.3
  286.9 0.8 copy-start.4
  294.1 2.0 copy-start.3
  297.5 0.8 copy-start.4
  304.8 2.0 copy-start.3
  308.1 0.8 copy-start.4
  315.4 2.0 copy-start.3
  318.8 0.8 copy-start.4
  325.9 2.0 copy-start
  329.3 0.8 copy-start.1
  336.5 2.0 copy-start
  339.8 0.8 copy-start.1
  347.0 2.0 copy-start
  350.4 0.8 copy-start.1
  357.5 2.0 copy-start
  360.9 0.8 copy-start.1
  368.0 2.0 copy-start
  371.4 0.8 copy-start.1
  378.6 2.0 copy-start
  381.9 0.8 copy-start.1
  382.8 30.8 %copy-start.2 = (f32[1,1024,128]{2,1,0:T(8,128)S(1)}, f32[1,1024,128]{2,1,0:T(8,128)}, u32[]{:S(2)}) copy-start(f32[1,1024,128]{2,1,0:T(8,128)} %get-tuple-element.708) | copy-start | bytes 1572868
  384.0 2.8 copy-start.5
  389.3 0.8 copy-start.6
  391.4 2.8 copy-start.5
  396.7 0.8 copy-start.6
  398.7 2.8 copy-start.5
  404.0 0.8 copy-start.6
  406.1 2.8 copy-start.5
  411.4 0.8 copy-start.6
  432.1 7.1 %copy-start.7 = (s32[2,32]{1,0:T(2,128)S(1)}, s32[2,32]{1,0:T(2,128)}, u32[]{:S(2)}) copy-start(s32[2,32]{1,0:T(2,128)} %param.24) | copy-start | bytes 772
Sparse Core Ops, SparseCore 0:
  11.5 113.1 all-gather.4
  128.2 127.5 all-gather.2
  439.3 35.8 reduce-scatter.1
where the time goes:
time: 483 us; the launch traced here: 482 us
  waiting for transfers between devices  273 us (57%)
  local copies, waits for them, and re-layouts  77.3 us (16%)
  matrix products  60.7 us (13%)
  other arithmetic  32.3 us (7%)
  loops' own time  23.8 us (5%)
  between operations  13.9 us (3%)
    all_gather x1, waiting for transfers between devices, shards(): pool_pages = lax.all_gather(kv_pool, 'pool', axis=0, tiled=True)  127 us
    all_gather x1, waiting for transfers between devices, shards(): gathered_new = lax.all_gather(new_kv, 'pool', axis=3, tiled=True)  113 us
    gather x12, local copies, waits for them, and re-layouts, prefix_step(): page_block = jnp.take(pool_pages, picked, axis=0)  41.2 us
    reduce_scatter x1, waiting for transfers between devices, shards(): lax.psum_scatter(partial_sums.astype(jnp.bfloat16), 'tp', scatter_dimensi...  32.3 us
    dot_general x20, matrix products, absorb(): jnp.einsum('grk,gkd->grd', weights.astype(jnp.bfloat16), value_rows, pref...  31.8 us
    dot_general x20, matrix products, absorb(): jnp.einsum('grd,gkd->grk', query_rows, key_rows, preferred_element_type=j...  21.8 us
    reduce_sum x20, other arithmetic, absorb(): row_total = row_total * factor + jnp.sum(weights, axis=2)  19.1 us
    another operation x2, loops' own time, shards(): lax.scan(prefix_step, start_state, jnp.arange(prefix_blocks, dtype=jnp.in...  17.9 us
  transfers between devices with their start and end apart: 3, of which 3 were waited for; matrix products, arithmetic and copies ran while one was open for 2% of the time, Pallas kernels for 0%

commit v1 on v0

v1 whole, which is shorter than its diff:
```python
import functools

import jax
import jax.numpy as jnp
from jax import lax
from jax.experimental import pallas as pl
from jax.experimental.pallas import tpu as pltpu
from jax.sharding import PartitionSpec as P

MESH = pl.DeviceIdType.MESH
F32 = jnp.float32
BF16 = jnp.bfloat16
NY, NX, NH, NZ, NC = 4, 4, 2, 4, 2
PAGE = 128
HD = 128
GROUP = 8
ROWS = GROUP * PAGE
HALF = 512
KB = 1024
LIVE = 64
FULL = 48
SCALE = 1.4426950408889634 / HD**0.5
LOW = -1e30


def dot_t(a, b):
    return lax.dot_general(a, b, (((1,), (1,)), ((), ())), preferred_element_type=F32)


def dot_0(a, b):
    return lax.dot_general(a, b, (((0,), (0,)), ((), ())), preferred_element_type=F32)


def body(
    tab, q_ref, new_ref, pool_ref, w_hbm, out_ref, dec_ref,
    pages, news, qs, scores, acc, m_ref, l_ref, w_ref, att,
    sib_out, sib_in, chip, line_out, line_in, res,
    send, recv, z_send, z_recv, s_send, s_recv, t_send, t_recv, w_sem,
):
    p = lax.axis_index("pool")
    t = lax.axis_index("tp")
    y, x, h = p // (NX * NH), (p // NH) % NX, p % NH
    zl, core = t // NC, t % NC

    def at(yy, xx, hh):
        return {"pool": ((yy % NY) * NX + xx % NX) * NH + hh, "tp": t}

    w_copy = pltpu.make_async_copy(w_hbm, w_ref, w_sem)
    w_copy.start()

    barrier = pltpu.get_barrier_semaphore()
    partners = [at(y, x + d, h) for d in (1, 2, 3)]
    partners += [at(y + d, x, h) for d in (1, 2, 3)]
    partners += [at(y, x, 1 - h)]
    partners += [{"pool": p, "tp": zl * NC + 1 - core}]
    partners += [{"pool": p, "tp": ((zl + d) % NZ) * NC + core} for d in (1, 2, 3)]
    for device in partners:
        pl.semaphore_signal(barrier, inc=1, device_id=device, device_id_type=MESH)

    full = tab[LIVE + 3]
    for r in range(2):
        source = full if r == 0 else 1 - full
        for kv in range(2):
            news[r, kv, y, x, h] = new_ref[source, 0, kv]
        for g in range(GROUP):
            qs[r, g * PAGE:(g + 1) * PAGE, :] = q_ref[source, :, g * HD:(g + 1) * HD]
    for s in range(2):
        pages[s, y, x, h] = pool_ref[tab[LIVE + s], 0]
    pl.semaphore_wait(barrier, len(partners))

    def copy(ref, device, send_sem, recv_sem):
        return pltpu.make_async_remote_copy(
            src_ref=ref, dst_ref=ref, send_sem=send_sem, recv_sem=recv_sem,
            device_id=device, device_id_type=MESH,
        )

    def stage(phase, which):
        if phase < 2:
            hh = h if phase == 0 else 1 - h
            a_ref = pages.at[0, y, x, hh] if which == 0 else pages.at[0, y, :, hh]
            b_ref = pages.at[1, y, x, hh] if which == 0 else pages.at[1, :, x, hh]
        else:
            r = phase - 2
            a_ref = news.at[r, 0, y, x] if which == 0 else news.at[r, 0, y]
            b_ref = news.at[r, 1, y, x] if which == 0 else news.at[r, 1, :, x]
        copies = []
        for d in (1, 3, 2):
            i = (phase * 2 + which) * 6 + (d - 1) * 2
            by_x, by_y = at(y, x + d, h), at(y + d, x, h)
            first, second = (by_x, by_y) if which == 0 else (by_y, by_x)
            copies.append(copy(a_ref, first, send.at[i], recv.at[i]))
            copies.append(copy(b_ref, second, send.at[i + 1], recv.at[i + 1]))
        return copies

    def start(copies):
        for one in copies:
            one.start()

    def arrived(copies):
        for one in copies:
            one.wait_recv()

    across = [
        copy(pages.at[:, y, x, h], at(y, x, 1 - h), z_send.at[0], z_recv.at[0]),
        copy(news.at[:, :, y, x, h], at(y, x, 1 - h), z_send.at[1], z_recv.at[1]),
    ]
    stages = [[stage(phase, which) for which in range(2)] for phase in range(4)]
    start(stages[0][0])
    start(across)
    acc[...] = jnp.zeros_like(acc)
    m_ref[...] = jnp.full_like(m_ref, LOW)
    l_ref[...] = jnp.zeros_like(l_ref)
    arrived(stages[0][0])
    start(stages[0][1])
    arrived(across[:1])
    start(stages[1][0])
    arrived(stages[1][0])
    start(stages[1][1])
    arrived(across[1:])
    arrived(stages[0][1])
    start(stages[2][0])
    arrived(stages[2][0])
    start(stages[2][1])
    arrived(stages[1][1])
    start(stages[3][0])

    def produce(r, slot, keys):
        scores[slot] = dot_t(keys, qs[r, slot * HALF:(slot + 1) * HALF, :])

    def consume(r, slot, values, mask):
        cols = slice(slot * HALF, (slot + 1) * HALF)
        s = scores[slot]
        if mask is not None:
            s = jnp.where(mask, s, LOW)
        old = m_ref[r, :1, cols]
        top = jnp.maximum(old, jnp.max(s, axis=0, keepdims=True))
        weights = jnp.exp2((s - top) * SCALE)
        factor = jnp.exp2((old - top) * SCALE)
        l_ref[r, :1, cols] = l_ref[r, :1, cols] * factor + jnp.sum(weights, axis=0, keepdims=True)
        acc[r, :, cols] = acc[r, :, cols] * factor + dot_0(values, weights.astype(BF16))
        m_ref[r, :1, cols] = top

    def run(r, first, last, load, mask=None):
        produce(r, 0, load(first, 0))

        def step(i, carry):
            produce(r, 1, load(i, 0))
            consume(r, 0, load(i, 1), mask)
            produce(r, 0, load(jnp.minimum(i + 1, last - 1), 0))
            consume(r, 1, load(i, 1), mask)
            return carry

        lax.fori_loop(first, last, step, 0)

    def prefix(base):
        def load(i, kv):
            parts = []
            for j in range(KB // PAGE):
                where = tab[base + i * (KB // PAGE) + j]
                owner = where // 2
                parts.append(pages[where % 2, owner // (NX * NH), (owner // NH) % NX, owner % NH, kv])
            return jnp.concatenate(parts, axis=0)

        return load

    def new(r):
        def load(i, kv):
            return news[r, kv, i].reshape(KB, HD)

        return load

    run(0, 0, 3, prefix(0))
    arrived(stages[3][0])
    start(stages[3][1])
    run(0, 3, 6, prefix(0))
    run(1, 0, 1, prefix(FULL))
    key_pos = lax.broadcasted_iota(jnp.int32, (KB, HALF), 0)
    run(1, 1, 2, prefix(FULL), key_pos < tab[LIVE + 2] - KB)

    row_tok = lax.broadcasted_iota(jnp.int32, (KB, HALF), 1) % PAGE
    causal = key_pos <= row_tok + (p % (NX * NH)) * PAGE
    finals = []
    for r in range(2):
        arrived(stages[2 + r][1])

        @pl.when(y > 0)
        def _():
            run(r, 0, y, new(r))

        run(r, y, y + 1, new(r), causal)

        mixed = (acc[r] / l_ref[r, :1, :]).astype(BF16)
        for g in range(GROUP):
            att[:, g * HD:(g + 1) * HD] = mixed[:, g * PAGE:(g + 1) * PAGE].T
        if r == 0:
            w_copy.wait()

        def columns(which):
            def part(j, carry):
                at_col = pl.multiple_of((j * NC + which) * 512, 512)
                got = jnp.dot(att[...], w_ref[:, pl.ds(at_col, 512)], preferred_element_type=F32)
                return got

            return part

        def to_sib(j, carry):
            sib_out[r, j] = columns(1 - core)(j, 0).astype(BF16)
            return carry

        def to_own(j, carry):
            chip[j] = columns(core)(j, 0)
            return carry

        lax.fori_loop(0, NZ, to_sib, 0)
        sib = pltpu.make_async_remote_copy(
            src_ref=sib_out.at[r], dst_ref=sib_in.at[r], send_sem=s_send.at[r], recv_sem=s_recv.at[r],
            device_id={"pool": p, "tp": zl * NC + 1 - core}, device_id_type=MESH,
        )
        sib.start()
        lax.fori_loop(0, NZ, to_own, 0)
        sib.wait_recv()
        line = []
        for d in (2, 1, 3):
            other = (zl + d) % NZ
            line_out[r, d - 1] = (chip[other] + sib_in[r, other].astype(F32)).astype(BF16)
            i = r * 3 + d - 1
            one = pltpu.make_async_remote_copy(
                src_ref=line_out.at[r, d - 1], dst_ref=line_in.at[r, d - 1],
                send_sem=t_send.at[i], recv_sem=t_recv.at[i],
                device_id={"pool": p, "tp": other * NC + core}, device_id_type=MESH,
            )
            one.start()
            line.append(one)
        res[r] = chip[zl] + sib_in[r, zl].astype(F32)
        finals.append((sib, line))
        if r == 0:
            continue
        for s in range(2):
            where = tab[LIVE + 4 + s]
            owner = where % (NY * NX * NH)
            side = jnp.where(where // (NY * NX * NH) == full, 0, 1)
            for kv in range(2):
                dec_ref[s, 0, kv] = news[side, kv, owner // (NX * NH), (owner // NH) % NX, owner % NH]

    for r in range(2):
        sib, line = finals[r]
        arrived(line)
        total = res[r]
        for d in range(3):
            total = total + line_in[r, d].astype(F32)
        res[r] = total
    out_ref[0] = res[full].astype(BF16)
    out_ref[1] = res[1 - full].astype(BF16)

    for phase in range(4):
        for which in range(2):
            for one in stages[phase][which]:
                one.wait_send()
    for one in across:
        one.wait_send()
    for sib, line in finals:
        sib.wait_send()
        for one in line:
            one.wait_send()


def shards(queries, new_kv, kv_pool, block_owner, block_slot, prefix_len, decode_page, out_weight):
    me = lax.axis_index("pool")
    entries = jnp.arange(block_owner.shape[1], dtype=jnp.int32)[None, :]
    dead = (entries * PAGE >= prefix_len[:, None]).reshape(-1)
    owner = block_owner.reshape(-1)
    slot = block_slot.reshape(-1)
    same = (owner[:, None] == owner[None, :]) & dead[None, :]
    hole = jnp.sum(jnp.where(same, slot[None, :], 0), axis=1)
    where = (owner * 2 + slot - (slot > hole).astype(jnp.int32)).reshape(2, -1)
    full = jnp.where(prefix_len[0] == FULL * PAGE, 0, 1).astype(jnp.int32)
    mine = jnp.sum(jnp.where(dead & (owner == me), slot, 0))
    is_first = full == 0
    long_list = jnp.where(is_first, where[0], where[1])
    short_list = jnp.where(is_first, where[1], where[0])[: LIVE - FULL]
    short_len = jnp.where(is_first, prefix_len[1], prefix_len[0])
    flat_page = decode_page.reshape(-1)
    index = jnp.arange(flat_page.shape[0], dtype=jnp.int32)
    source = [jnp.sum(jnp.where(flat_page == me * 2 + s, index, 0)) for s in range(2)]
    scalars = jnp.stack([jnp.where(mine == 0, 1, 0), jnp.where(mine == 2, 1, 2), short_len, full, *source])
    table = jnp.concatenate([long_list, short_list, scalars]).astype(jnp.int32)

    vmem = pl.BlockSpec(memory_space=pltpu.VMEM)
    out, dec = pl.pallas_call(
        body,
        out_shape=(
            jax.ShapeDtypeStruct((2, PAGE, 512), BF16),
            jax.ShapeDtypeStruct((2, 1, 2, PAGE, HD), BF16),
        ),
        in_specs=[pl.BlockSpec(memory_space=pltpu.SMEM), vmem, vmem, vmem, pl.BlockSpec(memory_space=pl.ANY)],
        out_specs=(vmem, vmem),
        scratch_shapes=[
            pltpu.VMEM((2, NY, NX, NH, 2, PAGE, HD), BF16),
            pltpu.VMEM((2, 2, NY, NX, NH, PAGE, HD), BF16),
            pltpu.VMEM((2, ROWS, HD), BF16),
            pltpu.VMEM((2, KB, HALF), F32),
            pltpu.VMEM((2, HD, ROWS), F32),
            pltpu.VMEM((2, 8, ROWS), F32),
            pltpu.VMEM((2, 8, ROWS), F32),
            pltpu.VMEM((GROUP * HD, 4096), BF16),
            pltpu.VMEM((PAGE, GROUP * HD), BF16),
            pltpu.VMEM((2, NZ, PAGE, 512), BF16),
            pltpu.VMEM((2, NZ, PAGE, 512), BF16),
            pltpu.VMEM((NZ, PAGE, 512), F32),
            pltpu.VMEM((2, 3, PAGE, 512), BF16),
            pltpu.VMEM((2, 3, PAGE, 512), BF16),
            pltpu.VMEM((2, PAGE, 512), F32),
            pltpu.SemaphoreType.DMA((48,)),
            pltpu.SemaphoreType.DMA((48,)),
            pltpu.SemaphoreType.DMA((2,)),
            pltpu.SemaphoreType.DMA((2,)),
            pltpu.SemaphoreType.DMA((2,)),
            pltpu.SemaphoreType.DMA((2,)),
            pltpu.SemaphoreType.DMA((6,)),
            pltpu.SemaphoreType.DMA((6,)),
            pltpu.SemaphoreType.DMA,
        ],
        compiler_params=pltpu.CompilerParams(
            collective_id=0, has_side_effects=True, vmem_limit_bytes=56 << 20
        ),
        cost_estimate=pl.CostEstimate(flops=11 * 10**9, bytes_accessed=10 << 20, transcendentals=16 << 20),
        name="paged_prefill",
    )(table, queries, new_kv, kv_pool, out_weight)
    return out, dec


def solution(mesh):
    return jax.shard_map(
        shards,
        mesh=mesh,
        in_specs=(
            P(None, "pool", "tp"),
            P(None, "tp", None, "pool", None),
            P("pool", "tp", None, None, None),
            P(),
            P(),
            P(),
            P(),
            P("tp", None),
        ),
        out_specs=(P(None, "pool", "tp"), P("pool", "tp", None, None, None)),
        check_vma=False,
    )
```

time: 483 us -> 119 us (0.25)
  waiting for transfers between devices: 273 us -> 0 us
  Pallas kernels: 0 us -> 102 us
  local copies, waits for them, and re-layouts: 77.3 us -> 7.99 us
  matrix products: 60.7 us -> 0 us
  other arithmetic: 32.3 us -> 3.04 us
  loops' own time: 23.8 us -> 0 us
  between operations: 13.9 us -> 3.92 us
    all_gather x2 -> x0, waiting for transfers between devices: 240 us -> none  [the longest x1 127 us: shards(): pool_pages = lax.all_gather(kv_pool, 'pool', axis=0, tiled=True)]
    pallas_call x0 -> x1, Pallas kernels: none -> 102 us  [shards(): pl.pallas_call(body, out_shape=(jax.ShapeDtypeStruct((2, PAGE, 512), BF16...]
    dot_general x41 -> x0, matrix products: 60.7 us -> none  [the longest x20 31.8 us: absorb(): jnp.einsum('grk,gkd->grd', weights.astype(jnp.bfloat16), value_rows, pref...]
    gather x13 -> x0, local copies, waits for them, and re-layouts: 44.6 us -> none  [the longest x12 41.2 us: prefix_step(): page_block = jnp.take(pool_pages, picked, axis=0)]
    reduce_scatter x1 -> x0, waiting for transfers between devices: 32.3 us -> none  [shards(): lax.psum_scatter(partial_sums.astype(jnp.bfloat16), 'tp', scatter_dimensi...]
    another operation x4 -> x0, loops' own time: 23.8 us -> none  [the longest x2 17.9 us: shards(): lax.scan(prefix_step, start_state, jnp.arange(prefix_blocks, dtype=jnp.in...]
    reduce_sum x21 -> x3, other arithmetic: 19.3 us -> 2.96 us  [the longest x1 1.4 us: shards(): mine = jnp.sum(jnp.where(dead & (owner == me), slot, 0))]
    while x84 -> x0, local copies, waits for them, and re-layouts: 12.9 us -> none
  transfers between devices with their start and end apart: 3 -> 0, of which waited for: 3 -> 0; matrix products, arithmetic and copies ran while one was open for 2% -> 0% of each run, Pallas kernels for 0% -> 0%
where the time goes in v1:
time: 119 us; the launch traced here: 117 us
  Pallas kernels  102 us (86%)
  local copies, waits for them, and re-layouts  7.99 us (7%)
  between operations  3.92 us (3%)
  other arithmetic  3.04 us (3%)
    pallas_call x1, Pallas kernels, shards(): pl.pallas_call(body, out_shape=(jax.ShapeDtypeStruct((2, PAGE, 512), BF16...  102 us
    unnamed x2, local copies, waits for them, and re-layouts  3.24 us

profile of v1, /device:TPU:24, one launch (start us, length us, event | category | flops | bytes accessed | tf_op | source)
XLA Modules:
  0.0 116.7 jit_solution(8855965253859498243)
XLA Ops:
  0.6 1.4 %fusion.2 = (s32[]{:T(128)}, s32[]{:T(128)}) fusion(s32[2,32]{1,0:T(2,128)} %param.14, s32[]{:T(128)S(6)} %add.9, s32[]{:T(128)S(6)} %mul.25), kind=kLoop, calls=%fused_computation.7 | loop fusion | flops 510 | bytes 272 | tf_op jit(solution)/shard_map/reduce_sum | solution.py:284
  2.0 0.8 reshape.44
  2.8 0.8 reshape.45
  3.5 1.4 %fusion = (s32[]{:T(128)}, pred[2,48]{1,0:T(4,128)(4,1)S(1)}) fusion(s32[2,48]{1,0:T(2,128)} %param.12, s32[2,48]{1,0:T(2,128)} %param.11, s32[]{:T(128)S(6)} %axis_index.15, s32[2]{0:T(128)} %param.13, s32[48]{0:T(128)S(1)} %iota_multiply_fusion), kind=kLoop, calls=%fused_computation.5 | loop fusion | flops 479 | bytes 1072 | tf_op jit(solution)/shard_map/reduce_sum | solution.py:277
  6.2 0.1 ge.25
  6.3 0.2 select_reduce_fusion
  6.5 1.3 %fusion.4 = (s32[1]{0:T(128)}, s32[1]{0:T(128)}) fusion(s32[2]{0:T(128)} %param.13), kind=kLoop, calls=%fused_computation.14 | loop fusion | bytes 16 | tf_op jit(solution)/shard_map/slice | solution.py:281
  9.8 0.1 broadcast_select_fusion
  9.9 1.8 %concatenate.3.tab = s32[70]{0:T(128)} concatenate(s32[48]{0:T(128)S(1)} %get-tuple-element.9, s32[16]{0:T(128)S(1)} %bitcast.9, s32[1]{0:T(128)} %bitcast.1, s32[1]{0:T(128)} %bitcast.2, s32[1]{0:T(128)} %bitcast.4, s32[1]{0:T(128)} %bitcast.5, s32[1]{0:T(128)} %bitcast.6, s32[1]{0:T(128)} %bitcast.7), dimensions={0} | concatenate | bytes 560 | tf_op jit(solution)/shard_map/concatenate | solution.py:286
  11.7 101.8 %paged_prefill.1 = (bf16[2,128,512]{2,1,0:T(8,128)(2,1)}, bf16[2,1,2,128,128]{4,3,2,1,0:T(8,128)(2,1)}) custom-call(s32[70]{0:T(128)} %concatenate.3.tab, bf16[2,128,1024]{2,1,0:T(8,128)(2,1)} %q_ref.1, bf16[2,1,2,128,128]{4,3,2,1,0:T(8,128)(2,1)} %new_ref.1, bf16[3,1,2,128,128]{4,3,2,1,0:T(8,128)(2,1)} %pool_ref.1, bf16[1024,4096]{1,0:T(8,128)(2,1)} %w_hbm.1), custom_call_target="tpu_custom_call" | custom-call | flops 11000000512 | bytes 10485760 | tf_op jit(solution)/shard_map/paged_prefill/pallas_call | solution.py:289
  113.5 1.7 %copy.12 = bf16[2,128,512]{2,1,0:T(8,128)(2,1)} copy(bf16[2,128,512]{2,1,0:T(8,128)(2,1)} %get-tuple-element.12) | data formatting | bytes 524288
  115.2 1.6 %copy.13 = bf16[2,1,2,128,128]{4,3,2,1,0:T(8,128)(2,1)} copy(bf16[2,1,2,128,128]{4,3,2,1,0:T(8,128)(2,1)} %get-tuple-element.13) | data formatting | bytes 262144
  (2 shorter events, 0.0 us)

commit v2 on v1

v2 whole, which is shorter than its diff:
```python
import functools

import jax
import jax.numpy as jnp
from jax import lax
from jax.experimental import pallas as pl
from jax.experimental.pallas import tpu as pltpu
from jax.sharding import PartitionSpec as P

MESH = pl.DeviceIdType.MESH
F32 = jnp.float32
BF16 = jnp.bfloat16
NY, NX, NH, NZ, NC = 4, 4, 2, 4, 2
PAGE = 128
HD = 128
GROUP = 8
ROWS = GROUP * PAGE
HALF = 512
KB = 1024
LIVE = 64
FULL = 48
SCALE = 1.4426950408889634 / HD**0.5
LOW = -1e30


def dot_t(a, b):
    return lax.dot_general(a, b, (((1,), (1,)), ((), ())), preferred_element_type=F32)


def dot_0(a, b):
    return lax.dot_general(a, b, (((0,), (0,)), ((), ())), preferred_element_type=F32)


def body(
    len_ref, own_ref, slot_ref, dpage_ref, q_hbm, new_ref, pool_ref, w_hbm, out_ref, dec_ref,
    near, far, news, q_v, qs, scores, acc, m_ref, l_ref, w_ref, att,
    sib_out, sib_in, line_out, line_in, res, tab_v, tab,
    send, recv, z_send, z_recv, s_send, s_recv, t_send, t_recv, w_sem, tab_sem, q_sem,
):
    p = lax.axis_index("pool")
    t = lax.axis_index("tp")
    y, x, h = p // (NX * NH), (p // NH) % NX, p % NH
    zl, core = t // NC, t % NC

    def at(yy, xx, hh):
        return {"pool": (((yy + NY) % NY) * NX + (xx + NX) % NX) * NH + hh, "tp": t}

    w_copy = pltpu.make_async_copy(w_hbm, w_ref, w_sem)
    w_copy.start()
    q_copy = pltpu.make_async_copy(q_hbm, q_v, q_sem)
    q_copy.start()

    barrier = pltpu.get_barrier_semaphore()
    partners = [at(y, x + d, h) for d in (1, 2, 3)]
    partners += [at(y + d, x, h) for d in (1, 2, 3)]
    partners += [at(y, x, 1 - h)]
    partners += [{"pool": p, "tp": zl * NC + 1 - core}]
    beside, opposite = zl + 1 - 2 * (zl % 2), (zl + 2) % NZ
    partners += [{"pool": p, "tp": z * NC + core} for z in (beside, opposite)]
    for device in partners:
        pl.semaphore_signal(barrier, inc=1, device_id=device, device_id_type=MESH)

    full = jnp.where(len_ref[0] == FULL * PAGE, 0, 1)
    short_len = len_ref[1 - full]

    entry = lax.broadcasted_iota(jnp.int32, (1, FULL), 1)
    device_row = lax.broadcasted_iota(jnp.int32, (NY * NX * NH, FULL), 0)
    owners = [own_ref[r:r + 1, :] for r in range(2)]
    slots = [slot_ref[r:r + 1, :] for r in range(2)]
    dead = [entry * PAGE >= len_ref[r] for r in range(2)]
    holes = jnp.zeros((NY * NX * NH, 1), jnp.int32)
    mine = jnp.int32(0)
    for r in range(2):
        dead_slot = jnp.where(dead[r], slots[r], 0)
        holes = holes + jnp.sum(jnp.where(owners[r] == device_row, dead_slot, 0), axis=1, keepdims=True)
        mine = mine + jnp.sum(jnp.where(owners[r] == p, dead_slot, 0))
    first_slot = jnp.where(mine == 0, 1, 0)
    second_slot = jnp.where(mine == 2, 1, 2)
    for s, chosen in enumerate((first_slot, second_slot)):
        near[s, y, x] = pool_ref[chosen, 0]

    def copy(ref, device, send_sem, recv_sem, there=None):
        return pltpu.make_async_remote_copy(
            src_ref=ref, dst_ref=ref if there is None else there, send_sem=send_sem, recv_sem=recv_sem,
            device_id=device, device_id_type=MESH,
        )

    def start(copies):
        for one in copies:
            one.start()

    def arrived(copies):
        for one in copies:
            one.wait_recv()

    def phase_copies(phase):
        if phase < 2:
            held = near if phase == 0 else far

            def a_item(yy, xx, part=None):
                ref = held.at[0, yy, xx]
                return ref if part is None else ref.at[part]

            def b_item(yy, xx, part=None):
                ref = held.at[1, yy, xx]
                return ref if part is None else ref.at[part]
        else:

            def a_item(yy, xx, part=None):
                ref = news.at[phase - 2, 0, yy, xx]
                return ref if part is None else ref.at[part]

            def b_item(yy, xx, part=None):
                ref = news.at[phase - 2, 1, yy, xx]
                return ref if part is None else ref.at[part]

        count = [phase * 40]

        def one(ref, device):
            i = count[0]
            count[0] += 1
            return copy(ref, device, send.at[i], recv.at[i])

        def wrap(v, n):
            return (v + n) % n

        steps = {}
        steps["s1"] = []
        for d in (1, 3, 2):
            steps["s1"] += [one(a_item(y, x), at(y, x + d, h)), one(b_item(y, x), at(y + d, x, h))]
        for k in range(4):
            xx, yy = wrap(x + k, NX), wrap(y + k, NY)
            steps["g%d" % k] = [
                one(a_item(y, xx), at(y + 1, x, h)), one(a_item(y, xx), at(y - 1, x, h)),
                one(b_item(yy, x), at(y, x + 1, h)), one(b_item(yy, x), at(y, x - 1, h)),
            ]
            steps["f2%d" % k] = [
                one(a_item(wrap(y - 1, NY), xx, 0), at(y + 1, x, h)),
                one(a_item(wrap(y + 1, NY), xx, 1), at(y - 1, x, h)),
                one(b_item(yy, wrap(x - 1, NX), 0), at(y, x + 1, h)),
                one(b_item(yy, wrap(x + 1, NX), 1), at(y, x - 1, h)),
            ]
        return steps

    phases = [phase_copies(phase) for phase in range(4)]
    across = [
        copy(near.at[:, y, x], at(y, x, 1 - h), z_send.at[0], z_recv.at[0], far.at[:, y, x]),
        copy(news.at[0, :, y, x, h], at(y, x, 1 - h), z_send.at[1], z_recv.at[1]),
        copy(news.at[1, :, y, x, h], at(y, x, 1 - h), z_send.at[2], z_recv.at[2]),
    ]

    def begin(n):
        if n > 0:
            arrived(across[n - 1:n])
        start(phases[n]["s1"])
        start(phases[n]["g0"])

    def event(n, what):
        ph = phases[n]
        if what == 0:
            arrived(ph["s1"])
            for k in (1, 3, 2):
                start(ph["g%d" % k])
        elif what < 5:
            k = (0, 1, 3, 2)[what - 1]
            arrived(ph["g%d" % k])
            start(ph["f2%d" % k])
        else:
            for k in range(4):
                arrived(ph["f2%d" % k])

    pl.semaphore_wait(barrier, len(partners))
    start(phases[0]["s1"])
    start(across[:1])
    start(phases[0]["g0"])
    for r in range(2):
        for kv in range(2):
            news[r, kv, y, x, h] = new_ref[full if r == 0 else 1 - full, 0, kv]
    start(across[1:])
    q_copy.wait()
    for r in range(2):
        source = full if r == 0 else 1 - full
        for g in range(GROUP):
            qs[r, g * PAGE:(g + 1) * PAGE, :] = q_v[source, :, g * HD:(g + 1) * HD]

    def turned(row):
        n = row.shape[1]
        rows = lax.broadcasted_iota(jnp.int32, (n, n), 0)
        lanes = lax.broadcasted_iota(jnp.int32, (n, n), 1)
        return jnp.sum(jnp.where(rows == lanes, row, 0), axis=1, keepdims=True)

    spots = []
    for r in range(2):
        hole = jnp.sum(jnp.where(owners[r] == device_row, holes, 0), axis=0, keepdims=True)
        spots.append((slots[r] - (slots[r] > hole).astype(jnp.int32)) * (NY * NX * NH) + owners[r])
    first_full = full == 0
    long_spots = jnp.where(first_full, spots[0], spots[1])
    short_spots = jnp.where(first_full, spots[1], spots[0])
    long_near = (long_spots % NH == h).astype(jnp.int32)
    near_col = turned(long_near)
    spot_col = turned(long_spots)
    rows = lax.broadcasted_iota(jnp.int32, (FULL, FULL), 0)
    lanes = lax.broadcasted_iota(jnp.int32, (FULL, FULL), 1)
    before_near = jnp.sum(jnp.where(lanes < rows, long_near, 0), axis=1, keepdims=True)
    all_near = jnp.sum(long_near, axis=1, keepdims=True)
    rank = jnp.where(near_col == 1, before_near, all_near + rows[:, :1] - before_near)
    ordered = jnp.sum(jnp.where(rank == lanes, spot_col, 0), axis=0, keepdims=True)
    tab_v[0:1, 0:FULL] = ordered
    tab_v[1:2, 0:FULL] = short_spots
    tab_copy = pltpu.make_async_copy(tab_v, tab, tab_sem)
    tab_copy.start()
    acc[...] = jnp.zeros_like(acc)
    m_ref[...] = jnp.full_like(m_ref, LOW)
    l_ref[...] = jnp.zeros_like(l_ref)

    def produce(r, slot, keys):
        scores[slot] = dot_t(keys, qs[r, slot * HALF:(slot + 1) * HALF, :])

    def consume(r, slot, values, mask):
        cols = slice(slot * HALF, (slot + 1) * HALF)
        s = scores[slot]
        if mask is not None:
            s = jnp.where(mask, s, LOW)
        old = m_ref[r, :1, cols]
        top = jnp.maximum(old, jnp.max(s, axis=0, keepdims=True))
        weights = jnp.exp2((s - top) * SCALE)
        factor = jnp.exp2((old - top) * SCALE)
        l_ref[r, :1, cols] = l_ref[r, :1, cols] * factor + jnp.sum(weights, axis=0, keepdims=True)
        acc[r, :, cols] = acc[r, :, cols] * factor + dot_0(values, weights.astype(BF16))
        m_ref[r, :1, cols] = top

    def run(blocks, services=()):
        services = list(services)
        halves = [(block, slot) for block in blocks for slot in range(2)]
        produce(halves[0][0][0], 0, halves[0][0][1](0))
        for n, ((r, load, mask), slot) in enumerate(halves):
            if n + 1 < len(halves):
                (r2, load2, mask2), slot2 = halves[n + 1]
                produce(r2, slot2, load2(0))
            consume(r, slot, load(1), mask)
            if services:
                for one in services.pop(0):
                    event(*one)
        assert not services

    def prefix(which, i, near_only=False):
        def load(kv):
            parts = []
            for j in range(KB // PAGE):
                where = tab[which, i * (KB // PAGE) + j]
                spot = (where // (NY * NX * NH), (where // (NX * NH)) % NY, (where // NH) % NX, kv)
                part = near[spot]
                if not near_only:
                    part = jnp.where(where % NH == h, part, far[spot])
                parts.append(part)
            return jnp.concatenate(parts, axis=0)

        return load

    def new(r, row):
        def load(kv):
            return news[r, kv, row].reshape(KB, HD)

        return load

    event(0, 0)
    begin(1)
    event(0, 1)
    event(0, 2)
    event(0, 3)
    event(1, 0)
    event(0, 4)
    tab_copy.wait()
    event(0, 5)
    begin(2)
    run([(0, prefix(0, i, True), None) for i in range(2)], [[(1, 1)], [(1, 2)], [(1, 3)], [(1, 4)]])
    event(2, 0)
    event(1, 5)
    begin(3)
    key_pos = lax.broadcasted_iota(jnp.int32, (KB, HALF), 0)
    row_tok = lax.broadcasted_iota(jnp.int32, (KB, HALF), 1) % PAGE
    in_short = key_pos < short_len - KB
    causal = key_pos <= row_tok + (p % (NX * NH)) * PAGE
    run(
        [(0, prefix(0, i), None) for i in range(2, 6)] + [(1, prefix(1, 0), None), (1, prefix(1, 1), in_short)],
        [[], [(2, 1)], [], [(2, 2)], [], [(2, 3)], [], [(2, 4)], [], [(3, 0)], [], [(3, 1)]],
    )

    finals = []
    for r in range(2):
        event(2 + r, 5)
        run([(r, new(r, y), causal)], [[], [(3, 2)]] if r == 0 else [])
        if r == 1:
            finals[0][2]()
        for k in (1, 2, 3):

            @pl.when(y >= k)
            def _():
                run([(r, new(r, y - k), None)])

            if r == 0 and k < 3:
                event(3, 2 + k)

        mixed = (acc[r] / l_ref[r, :1, :]).astype(BF16)
        for g in range(GROUP):
            att[:, g * HD:(g + 1) * HD] = mixed[:, g * PAGE:(g + 1) * PAGE].T
        if r == 0:
            w_copy.wait()

        def block(j, which):
            at_col = pl.multiple_of((j * NC + which) * 512, 512)
            return jnp.dot(att[...], w_ref[:, pl.ds(at_col, 512)], preferred_element_type=F32)

        dests = [NZ - 1 - zl, beside, opposite, zl]
        sibs, line = [], []

        def give(n):
            i = r * NZ + n
            sib_out[i] = block(dests[n], 1 - core).astype(BF16)
            one = pltpu.make_async_remote_copy(
                src_ref=sib_out.at[i], dst_ref=sib_in.at[i], send_sem=s_send.at[i], recv_sem=s_recv.at[i],
                device_id={"pool": p, "tp": zl * NC + 1 - core}, device_id_type=MESH,
            )
            one.start()
            sibs.append(one)

        def send_line(n, device, r=r, line=line):
            i = r * NZ + n
            one = pltpu.make_async_remote_copy(
                src_ref=line_out.at[i], dst_ref=line_in.at[i], send_sem=t_send.at[i], recv_sem=t_recv.at[i],
                device_id={"pool": p, "tp": device * NC + core}, device_id_type=MESH,
            )
            one.start()
            line.append(one)

        def pass_on(n):
            total = block(dests[n], core)
            sibs[n].wait_recv()
            total = total + sib_in[r * NZ + n].astype(F32)
            if n < 2:
                line_out[r * NZ + n] = total.astype(BF16)
                send_line(n, beside)
            else:
                res[r, n - 2] = total

        def relay(r=r, line=line, send_line=send_line):
            line[0].wait_recv()
            line_out[r * NZ + 2] = (res[r, 0] + line_in[r * NZ].astype(F32)).astype(BF16)
            send_line(2, opposite)

        give(0)
        give(1)
        pass_on(0)
        give(2)
        pass_on(1)
        give(3)
        pass_on(2)
        if r == 1:
            relay()
        pass_on(3)
        finals.append((sibs, line, relay))
        if r == 0:
            continue
        page_at = lax.broadcasted_iota(jnp.int32, dpage_ref.shape, 1)
        page_of = lax.broadcasted_iota(jnp.int32, dpage_ref.shape, 0)
        for s in range(2):
            chosen = dpage_ref[...] == p * 2 + s
            owner = jnp.minimum(jnp.sum(jnp.where(chosen, page_at, 0)), NY * NX * NH - 1)
            side = jnp.where(jnp.sum(jnp.where(chosen, page_of, 0)) == full, 0, 1)
            for kv in range(2):
                dec_ref[s, 0, kv] = news[side, kv, owner // (NX * NH), (owner // NH) % NX, owner % NH]

    for r in range(2):
        sibs, line, _ = finals[r]
        arrived(line[1:])
        res[r, 1] = res[r, 1] + line_in[r * NZ + 1].astype(F32) + line_in[r * NZ + 2].astype(F32)
    out_ref[0] = res[full, 1].astype(BF16)
    out_ref[1] = res[1 - full, 1].astype(BF16)

    for ph in phases:
        for copies in ph.values():
            for one in copies:
                one.wait_send()
    for one in across:
        one.wait_send()
    for sibs, line, _ in finals:
        for one in sibs + line:
            one.wait_send()


def shards(queries, new_kv, kv_pool, block_owner, block_slot, prefix_len, decode_page, out_weight):
    vmem = pl.BlockSpec(memory_space=pltpu.VMEM)
    any_space = pl.BlockSpec(memory_space=pl.ANY)
    out, dec = pl.pallas_call(
        body,
        out_shape=(
            jax.ShapeDtypeStruct((2, PAGE, 512), BF16),
            jax.ShapeDtypeStruct((2, 1, 2, PAGE, HD), BF16),
        ),
        in_specs=[pl.BlockSpec(memory_space=pltpu.SMEM)] + [vmem] * 3 + [any_space] + [vmem] * 2 + [any_space],
        out_specs=(vmem, vmem),
        scratch_shapes=[
            pltpu.VMEM((2, NY, NX, 2, PAGE, HD), BF16),
            pltpu.VMEM((2, NY, NX, 2, PAGE, HD), BF16),
            pltpu.VMEM((2, 2, NY, NX, NH, PAGE, HD), BF16),
            pltpu.VMEM((2, PAGE, GROUP * HD), BF16),
            pltpu.VMEM((2, ROWS, HD), BF16),
            pltpu.VMEM((2, KB, HALF), F32),
            pltpu.VMEM((2, HD, ROWS), F32),
            pltpu.VMEM((2, 8, ROWS), F32),
            pltpu.VMEM((2, 8, ROWS), F32),
            pltpu.VMEM((GROUP * HD, 4096), BF16),
            pltpu.VMEM((PAGE, GROUP * HD), BF16),
            pltpu.VMEM((2 * NZ, PAGE, 512), BF16),
            pltpu.VMEM((2 * NZ, PAGE, 512), BF16),
            pltpu.VMEM((2 * NZ, PAGE, 512), BF16),
            pltpu.VMEM((2 * NZ, PAGE, 512), BF16),
            pltpu.VMEM((2, 2, PAGE, 512), F32),
            pltpu.VMEM((8, 128), jnp.int32),
            pltpu.SMEM((8, 128), jnp.int32),
            pltpu.SemaphoreType.DMA((160,)),
            pltpu.SemaphoreType.DMA((160,)),
            pltpu.SemaphoreType.DMA((3,)),
            pltpu.SemaphoreType.DMA((3,)),
            pltpu.SemaphoreType.DMA((8,)),
            pltpu.SemaphoreType.DMA((8,)),
            pltpu.SemaphoreType.DMA((8,)),
            pltpu.SemaphoreType.DMA((8,)),
            pltpu.SemaphoreType.DMA,
            pltpu.SemaphoreType.DMA,
            pltpu.SemaphoreType.DMA,
        ],
        compiler_params=pltpu.CompilerParams(
            collective_id=0, has_side_effects=True, vmem_limit_bytes=56 << 20
        ),
        cost_estimate=pl.CostEstimate(flops=11 * 10**9, bytes_accessed=10 << 20, transcendentals=16 << 20),
        name="paged_prefill",
    )(prefix_len, block_owner, block_slot, decode_page, queries, new_kv, kv_pool, out_weight)
    return out, dec


def solution(mesh):
    return jax.shard_map(
        shards,
        mesh=mesh,
        in_specs=(
            P(None, "pool", "tp"),
            P(None, "tp", None, "pool", None),
            P("pool", "tp", None, None, None),
            P(),
            P(),
            P(),
            P(),
            P("tp", None),
        ),
        out_specs=(P(None, "pool", "tp"), P("pool", "tp", None, None, None)),
        check_vma=False,
    )
```

time: 119 us -> 95.3 us (0.80); the launches traced: 117 us -> 95.2 us
  Pallas kernels: 102 us -> 91.3 us
  local copies, waits for them, and re-layouts: 7.99 us -> 3.24 us
  between operations: 3.92 us -> 0.64 us
  other arithmetic: 3.04 us -> 0 us
    pallas_call x1, Pallas kernels: 102 us -> 91.3 us  [shards(): pl.pallas_call(body, out_shape=(jax.ShapeDtypeStruct((2, PAGE, 512), BF16...]
    reduce_sum x3 -> x0, other arithmetic: 2.96 us -> none  [the longest x1 1.4 us: shards(): mine = jnp.sum(jnp.where(dead & (owner == me), slot, 0))]
    concatenate x1 -> x0, local copies, waits for them, and re-layouts: 1.84 us -> none  [shards(): table = jnp.concatenate([long_list, short_list, scalars]).astype(jnp.int32)]
    reshape x2 -> x0, local copies, waits for them, and re-layouts: 1.52 us -> none  [the longest x1 0.76 us: shards(): owner = block_owner.reshape(-1)]
    slice x1 -> x0, local copies, waits for them, and re-layouts: 1.32 us -> none  [shards(): short_len = jnp.where(is_first, prefix_len[1], prefix_len[0])]
where the time goes in v2:
time: 95.3 us; the launch traced here: 95.2 us
  Pallas kernels  91.3 us (96%)
  local copies, waits for them, and re-layouts  3.24 us (3%)
    pallas_call x1, Pallas kernels, shards(): pl.pallas_call(body, out_shape=(jax.ShapeDtypeStruct((2, PAGE, 512), BF16...  91.3 us
    unnamed x2, local copies, waits for them, and re-layouts  3.24 us

profile of v2, /device:TPU:24, one launch (start us, length us, event | category | flops | bytes accessed | tf_op | source)
XLA Modules:
  0.0 95.2 jit_solution(18446671100080283925)
XLA Ops:
  0.6 91.3 %paged_prefill.1 = (bf16[2,128,512]{2,1,0:T(8,128)(2,1)}, bf16[2,1,2,128,128]{4,3,2,1,0:T(8,128)(2,1)}) custom-call(s32[2]{0:T(128)} %len_ref.1, s32[2,48]{1,0:T(2,128)} %own_ref.1, s32[2,48]{1,0:T(2,128)} %slot_ref.1, s32[2,32]{1,0:T(2,128)} %dpage_ref.1, bf16[2,128,1024]{2,1,0:T(8,128)(2,1)} %q_hbm.1, bf16[2,1,2,128,128]{4,3,2,1,0:T(8,128)(2,1)} %new_ref.1, ...), custom_call_target="tpu_custom_call" | custom-call | flops 11000000512 | bytes 10485760 | tf_op jit(solution)/shard_map/paged_prefill/pallas_call | solution.py:394
  91.9 1.7 %copy.12 = bf16[2,128,512]{2,1,0:T(8,128)(2,1)} copy(bf16[2,128,512]{2,1,0:T(8,128)(2,1)} %get-tuple-element.4) | data formatting | bytes 524288
  93.6 1.6 %copy.13 = bf16[2,1,2,128,128]{4,3,2,1,0:T(8,128)(2,1)} copy(bf16[2,1,2,128,128]{4,3,2,1,0:T(8,128)(2,1)} %get-tuple-element.5) | data formatting | bytes 262144

commit v3 on v2

--- a/solution.py
+++ b/solution.py
@@ -370,19 +370,19 @@
             for kv in range(2):
                 dec_ref[s, 0, kv] = news[side, kv, owner // (NX * NH), (owner // NH) % NX, owner % NH]
 
-    for r in range(2):
-        sibs, line, _ = finals[r]
-        arrived(line[1:])
-        res[r, 1] = res[r, 1] + line_in[r * NZ + 1].astype(F32) + line_in[r * NZ + 2].astype(F32)
-    out_ref[0] = res[full, 1].astype(BF16)
-    out_ref[1] = res[1 - full, 1].astype(BF16)
-
     for ph in phases:
         for copies in ph.values():
             for one in copies:
                 one.wait_send()
     for one in across:
         one.wait_send()
+    for r in range(2):
+        sibs, line, _ = finals[r]
+        arrived(line[1:])
+        res[r, 1] = res[r, 1] + line_in[r * NZ + 1].astype(F32) + line_in[r * NZ + 2].astype(F32)
+    out_ref[0] = res[full, 1].astype(BF16)
+    out_ref[1] = res[1 - full, 1].astype(BF16)
+
     for sibs, line, _ in finals:
         for one in sibs + line:
             one.wait_send()

time: 95.3 us -> 95.1 us (level)
  no operation moved by 1% of the time
where the time goes in v3:
time: 95.1 us; the launch traced here: 94.9 us
  Pallas kernels  91.1 us (96%)
  local copies, waits for them, and re-layouts  3.24 us (3%)
    pallas_call x1, Pallas kernels, shards(): pl.pallas_call(body, out_shape=(jax.ShapeDtypeStruct((2, PAGE, 512), BF16...  91.1 us
    unnamed x2, local copies, waits for them, and re-layouts  3.24 us

profile of v3, /device:TPU:24, one launch (start us, length us, event | category | flops | bytes accessed | tf_op | source)
XLA Modules:
  0.0 94.9 jit_solution(10993516642806039851)
XLA Ops:
  0.6 91.1 %paged_prefill.1 = (bf16[2,128,512]{2,1,0:T(8,128)(2,1)}, bf16[2,1,2,128,128]{4,3,2,1,0:T(8,128)(2,1)}) custom-call(s32[2]{0:T(128)} %len_ref.1, s32[2,48]{1,0:T(2,128)} %own_ref.1, s32[2,48]{1,0:T(2,128)} %slot_ref.1, s32[2,32]{1,0:T(2,128)} %dpage_ref.1, bf16[2,128,1024]{2,1,0:T(8,128)(2,1)} %q_hbm.1, bf16[2,1,2,128,128]{4,3,2,1,0:T(8,128)(2,1)} %new_ref.1, ...), custom_call_target="tpu_custom_call" | custom-call | flops 11000000512 | bytes 10485760 | tf_op jit(solution)/shard_map/paged_prefill/pallas_call | solution.py:394
  91.7 1.7 %copy.12 = bf16[2,128,512]{2,1,0:T(8,128)(2,1)} copy(bf16[2,128,512]{2,1,0:T(8,128)(2,1)} %get-tuple-element.4) | data formatting | bytes 524288
  93.4 1.6 %copy.13 = bf16[2,1,2,128,128]{4,3,2,1,0:T(8,128)(2,1)} copy(bf16[2,1,2,128,128]{4,3,2,1,0:T(8,128)(2,1)} %get-tuple-element.5) | data formatting | bytes 262144
